TPU v7x, 32 devices: a whole 2x2x4 slice. The times are simulated.
32 devices in a mesh: section: 4 (over y, x), dp: 8 (over z, core).
Axes of the slice: x: 2, y: 2, z: 4, core: 2. Of those that a mesh axis runs over, the one named last changes fastest.
Arguments:
- latents: bfloat16 [4, 8, 4, 16, 8, 256], P(None, 'dp'), may hold values from -36 to 36
- cotangent: bfloat16 [4, 8, 4, 16, 8, 256], P(None, 'dp'), may hold values from -6 to 6
- spatial_kernels: bfloat16 [4, 2304, 256], P('section'), may hold values from -0.125 to 0.125
- temporal_kernels: bfloat16 [4, 768, 256], P('section'), may hold values from -0.21875 to 0.21875
Outputs:
- grad_spatial: float32 [4, 2304, 256], P('section', 'dp')
- grad_temporal: float32 [4, 768, 256], P('section', 'dp')
All inputs are finite; a program needn't handle non-finite values.
Results may differ from a plain program's by a relative error of at most 0.017.
Values may be sent and summed in bfloat16 or wider, within the bound.
A program may use at most 128 MiB of HBM per device.

v0:
```python
import functools
import math

import jax
import jax.numpy as jnp
from jax import lax
from jax.experimental import pallas as pl
from jax.experimental.pallas import tpu as pltpu
from jax.sharding import PartitionSpec as P

MESH = pl.DeviceIdType.MESH
PER = 2


def slope_of(value, sig):
    return sig * (1.0 + value * (1.0 - sig))


def inv_rms_of(x):
    return lax.rsqrt(jnp.mean(x * x, axis=-1, keepdims=True) + 1e-06)


def column_shift(value, width, offset):
    cut = value.reshape(-1, width, value.shape[-1])
    col = lax.broadcasted_iota(jnp.int32, cut.shape, 1)
    rolled = pltpu.roll(cut, (-offset) % width, axis=1)
    edge = width - 1 if offset > 0 else 0
    return jnp.where(col == edge, 0.0, rolled).reshape(value.shape)


def dot(a, b):
    return jnp.dot(a, b, preferred_element_type=jnp.float32)


def kernel(
    dims,
    lat_ref, cot_ref, ws_ref, wt_ref,
    ds_ref, dt_ref,
    fwd_in, fwd_out, bwd_in, bwd_out,
    slope1, slope2, s1_t, s2_t, ws_t, wt_t,
    cols1, cols2, grads1, grads2, s2_prev, g_next, mixed, acc,
    f_send, f_recv, b_send, b_recv,
):
    micros, chunks, height, width, ch, sections = dims
    rows = height * PER * width
    line = PER * width
    total = micros * chunks
    sec = lax.axis_index("section")
    first = sec == 0
    last = sec == sections - 1

    barrier = pltpu.get_barrier_semaphore()

    @pl.when(jnp.logical_not(first))
    def _():
        pl.semaphore_signal(barrier, inc=1, device_id={"section": sec - 1}, device_id_type=MESH)

    @pl.when(jnp.logical_not(last))
    def _():
        pl.semaphore_signal(barrier, inc=1, device_id={"section": sec + 1}, device_id_type=MESH)

    acc[...] = jnp.zeros_like(acc)
    edge_rows = jnp.zeros((line, 3 * ch), jnp.bfloat16)
    cols1[0:line, :] = edge_rows
    cols1[line + rows : 2 * line + rows, :] = edge_rows
    for slot in range(chunks):
        grads1[slot, 0:line, :] = edge_rows
        grads1[slot, line + rows : 2 * line + rows, :] = edge_rows
    s2_prev[...] = jnp.zeros_like(s2_prev)
    g_next[...] = jnp.zeros_like(g_next)

    @pl.when(first | last)
    def _():
        pl.semaphore_wait(barrier, 1)

    @pl.when(jnp.logical_not(first | last))
    def _():
        pl.semaphore_wait(barrier, 2)

    def f_copy(k):
        return pltpu.make_async_remote_copy(
            src_ref=fwd_out.at[k], dst_ref=fwd_in.at[k],
            send_sem=f_send.at[k], recv_sem=f_recv.at[k],
            device_id={"section": sec + 1}, device_id_type=MESH,
        )

    def b_copy(k):
        return pltpu.make_async_remote_copy(
            src_ref=bwd_out.at[k], dst_ref=bwd_in.at[k],
            send_sem=b_send.at[k], recv_sem=b_recv.at[k],
            device_id={"section": sec - 1}, device_id_type=MESH,
        )

    def arrange(source, m, c, target, k):
        for f in range(PER):
            mixed[:, f] = source[m, c * PER + f].astype(jnp.float32)
        target[k] = mixed[...].reshape(rows, ch).astype(jnp.bfloat16)

    def forward(k):
        m, c = k // chunks, k % chunks

        @pl.when(first)
        def _():
            arrange(lat_ref, m, c, fwd_in, k)

        @pl.when(jnp.logical_not(first))
        def _():
            f_copy(k).wait_recv()

        x = fwd_in[k].astype(jnp.float32)
        u = x * inv_rms_of(x)
        sig = jax.nn.sigmoid(u)
        s1 = u * sig
        slope1[k] = slope_of(u, sig)
        s1b = s1.astype(jnp.bfloat16)
        cols1[line : line + rows, 0:ch] = column_shift(s1, width, -1).astype(jnp.bfloat16)
        cols1[line : line + rows, ch : 2 * ch] = s1b
        cols1[line : line + rows, 2 * ch : 3 * ch] = column_shift(s1, width, 1).astype(jnp.bfloat16)
        v = dot(cols1[0:rows, :], ws_ref[0 : 3 * ch, :])
        v += dot(cols1[line : line + rows, :], ws_ref[3 * ch : 6 * ch, :])
        v += dot(cols1[2 * line : 2 * line + rows, :], ws_ref[6 * ch : 9 * ch, :])
        sig2 = jax.nn.sigmoid(v)
        s2 = v * sig2
        slope2[k] = slope_of(v, sig2)
        s2b = s2.astype(jnp.bfloat16)

        @pl.when(jnp.logical_not(last))
        def _():
            now = s2.reshape(height, PER, width, ch)
            before = jnp.where(c == 0, 0.0, s2_prev[...])
            shifted = jnp.concatenate([before[:, 1:], now[:, :1]], axis=1)
            cols2[:, 0:ch] = before.reshape(rows, ch).astype(jnp.bfloat16)
            cols2[:, ch : 2 * ch] = shifted.reshape(rows, ch).astype(jnp.bfloat16)
            cols2[:, 2 * ch : 3 * ch] = s2b
            s2_prev[...] = now
            z = dot(cols2[...], wt_ref[...])
            fwd_out[k] = (x + z).astype(jnp.bfloat16)
            f_copy(k).start()

        s1_t[k] = s1b.T
        s2_t[k] = s2b.T

    def backward(j):
        m, c = j // chunks, chunks - 1 - j % chunks
        k = m * chunks + c

        @pl.when(last)
        def _():
            arrange(cot_ref, m, c, bwd_in, k)

        @pl.when(jnp.logical_not(last))
        def _():
            b_copy(k).wait_recv()

        gb = bwd_in[k]
        g = gb.astype(jnp.float32)
        now = g.reshape(height, PER, width, ch)
        after = jnp.where(c == chunks - 1, 0.0, g_next[...])
        shifted = jnp.concatenate([now[:, 1:], after[:, :1]], axis=1)
        grads2[c, :, 0:ch] = after.reshape(rows, ch).astype(jnp.bfloat16)
        grads2[c, :, ch : 2 * ch] = shifted.reshape(rows, ch).astype(jnp.bfloat16)
        grads2[c, :, 2 * ch : 3 * ch] = gb
        g_next[...] = now
        gmid = dot(grads2[c], wt_t[...]) * slope2[k]
        grads1[c, line : line + rows, 0:ch] = column_shift(gmid, width, 1).astype(jnp.bfloat16)
        grads1[c, line : line + rows, ch : 2 * ch] = gmid.astype(jnp.bfloat16)
        grads1[c, line : line + rows, 2 * ch : 3 * ch] = column_shift(gmid, width, -1).astype(jnp.bfloat16)

        @pl.when(jnp.logical_not(first))
        def _():
            back = dot(grads1[c, 2 * line : 2 * line + rows, :], ws_t[0 : 3 * ch, :])
            back += dot(grads1[c, line : line + rows, :], ws_t[3 * ch : 6 * ch, :])
            back += dot(grads1[c, 0:rows, :], ws_t[6 * ch : 9 * ch, :])
            gu = back * slope1[k]
            x = fwd_in[k].astype(jnp.float32)
            inv = inv_rms_of(x)
            gx = inv * gu - x * (inv * inv * inv) * jnp.mean(gu * x, axis=-1, keepdims=True)
            bwd_out[k] = (g + gx).astype(jnp.bfloat16)
            b_copy(k).start()

        @pl.when(c == 0)
        def _():
            for dr in range(3):
                top = (2 - dr) * line
                part = dot(s1_t[m * chunks], grads1[0, top : top + rows, :])
                for other in range(1, chunks):
                    part += dot(s1_t[m * chunks + other], grads1[other, top : top + rows, :])
                for dc in range(3):
                    acc[dr * 3 + dc] += part[:, dc * ch : (dc + 1) * ch]
            part = dot(s2_t[m * chunks], grads2[0])
            for other in range(1, chunks):
                part += dot(s2_t[m * chunks + other], grads2[other])
            for tap in range(3):
                acc[9 + tap] += part[:, tap * ch : (tap + 1) * ch]

    lag = chunks - 1 + 2 * (sections - 1)

    def tick(t, carry):
        i = t - sec

        @pl.when((i >= 0) & (i < total))
        def _():
            forward(i)

        @pl.when(t == jnp.where(first, sections - 1, 0))
        def _():
            for tap in range(9):
                ws_t[tap * ch : (tap + 1) * ch, :] = ws_ref[tap * ch : (tap + 1) * ch, :].T
            for tap in range(3):
                wt_t[tap * ch : (tap + 1) * ch, :] = wt_ref[tap * ch : (tap + 1) * ch, :].T

        j = t - (lag - sec)

        @pl.when((j >= 0) & (j < total))
        def _():
            backward(j)

        return carry

    lax.fori_loop(0, lag + total, tick, 0)

    for tap in range(9):
        ds_ref[tap * ch : (tap + 1) * ch, :] = acc[tap].astype(jnp.bfloat16)
    for tap in range(3):
        dt_ref[tap * ch : (tap + 1) * ch, :] = acc[9 + tap].astype(jnp.bfloat16)

    @pl.when(jnp.logical_not(last))
    def _():
        for k in range(total):
            f_copy(k).wait_send()

    @pl.when(jnp.logical_not(first))
    def _():
        for k in range(total):
            b_copy(k).wait_send()


def local(latents, cotangent, spatial_kernels, temporal_kernels):
    micros, crops, frames, height, width, ch = latents.shape
    sections = lax.axis_size("section")
    replicas = lax.axis_size("dp")
    chunks = frames // PER
    rows = height * PER * width
    line = PER * width
    total = micros * chunks
    vmem = pl.BlockSpec(memory_space=pltpu.VMEM)
    bf, f32 = jnp.bfloat16, jnp.float32
    hold_space, hold_time = pl.pallas_call(
        functools.partial(kernel, (micros, chunks, height, width, ch, sections)),
        out_shape=(
            jax.ShapeDtypeStruct((9 * ch, ch), bf),
            jax.ShapeDtypeStruct((3 * ch, ch), bf),
        ),
        in_specs=[vmem] * 4,
        out_specs=(vmem, vmem),
        scratch_shapes=[
            pltpu.VMEM((total, rows, ch), bf),
            pltpu.VMEM((total, rows, ch), bf),
            pltpu.VMEM((total, rows, ch), bf),
            pltpu.VMEM((total, rows, ch), bf),
            pltpu.VMEM((total, rows, ch), f32),
            pltpu.VMEM((total, rows, ch), f32),
            pltpu.VMEM((total, ch, rows), bf),
            pltpu.VMEM((total, ch, rows), bf),
            pltpu.VMEM((9 * ch, ch), bf),
            pltpu.VMEM((3 * ch, ch), bf),
            pltpu.VMEM((rows + 2 * line, 3 * ch), bf),
            pltpu.VMEM((rows, 3 * ch), bf),
            pltpu.VMEM((chunks, rows + 2 * line, 3 * ch), bf),
            pltpu.VMEM((chunks, rows, 3 * ch), bf),
            pltpu.VMEM((height, PER, width, ch), f32),
            pltpu.VMEM((height, PER, width, ch), f32),
            pltpu.VMEM((height, PER, width, ch), f32),
            pltpu.VMEM((12, ch, ch), f32),
            pltpu.SemaphoreType.DMA((total,)),
            pltpu.SemaphoreType.DMA((total,)),
            pltpu.SemaphoreType.DMA((total,)),
            pltpu.SemaphoreType.DMA((total,)),
        ],
        compiler_params=pltpu.CompilerParams(
            collective_id=0, has_side_effects=True, vmem_limit_bytes=48 * 1024 * 1024
        ),
    )(latents[:, 0], cotangent[:, 0], spatial_kernels[0], temporal_kernels[0])
    share_space = lax.psum_scatter(hold_space, "dp", scatter_dimension=0, tiled=True).astype(f32)
    share_time = lax.psum_scatter(hold_time, "dp", scatter_dimension=0, tiled=True).astype(f32)
    cells = micros * replicas * crops * frames * height * width
    grad_scale = 1.0 / math.sqrt(cells)
    return ((grad_scale * share_space)[None], (grad_scale * share_time)[None])


def solution(mesh):
    in_specs = (
        P(None, "dp", None, None, None, None),
        P(None, "dp", None, None, None, None),
        P("section", None, None),
        P("section", None, None),
    )
    out_specs = (P("section", "dp", None), P("section", "dp", None))
    return jax.shard_map(local, mesh=mesh, in_specs=in_specs, out_specs=out_specs, check_vma=False)
```

profile of v0, /device:TPU:0, one launch (start us, length us, event | category | flops | bytes accessed | tf_op | source)
XLA Modules:
  0.0 158.5 jit_solution(12934126524031636857)
XLA Ops:
  7.2 0.0 reduce-scatter.5.cloned.1.call-start
  7.2 0.0 copy-start
  7.2 1.3 copy-done
  8.5 0.0 copy-start.1
  8.5 1.2 copy-done.1
  9.7 0.0 copy-start.2
  9.7 1.2 copy-done.2
  10.9 0.0 copy-start.3
  10.9 1.0 copy-done.3
  11.9 74.7 %shard_map.59 = (bf16[2304,256]{1,0:T(8,128)(2,1)}, bf16[768,256]{1,0:T(8,128)(2,1)}) custom-call(bf16[4,4,16,8,256]{4,3,2,1,0:T(8,128)(2,1)S(1)} %bitcast.9, bf16[4,4,16,8,256]{4,3,2,1,0:T(8,128)(2,1)S(1)} %bitcast.10, bf16[2304,256]{1,0:T(8,128)(2,1)S(1)} %bitcast.8, bf16[768,256]{1,0:T(8,128)(2,1)S(1)} %bitcast.11), custom_call_target="tpu_custom_call" | custom-call | tf_op jit(solution)/shard_map/pallas_call | solution.py:248
  86.6 0.0 reduce-scatter.5.cloned.1.call-update
  86.6 0.0 reduce-scatter.3.cloned.1.call-start
  86.7 0.7 reduce-scatter.3.cloned.1.call-update
  87.4 29.4 %reduce-scatter.5.cloned.1.call-done = bf16[96,256]{1,0:T(8,128)(2,1)} async-done(((bf16[768,256]{1,0:T(8,128)(2,1)}), bf16[96,256]{1,0:T(8,128)(2,1)}) %reduce-scatter.5.cloned.1.call-update) | async-done | bytes 49168 | tf_op jit(solution)/shard_map/reduce_scatter | solution.py:285
  116.7 1.4 multiply_bitcast_fusion.1
  118.2 31.9 %reduce-scatter.3.cloned.1.call-done = bf16[288,256]{1,0:T(8,128)(2,1)} async-done(((bf16[2304,256]{1,0:T(8,128)(2,1)}), bf16[288,256]{1,0:T(8,128)(2,1)}) %reduce-scatter.3.cloned.1.call-update) | async-done | bytes 147472 | tf_op jit(solution)/shard_map/reduce_scatter | solution.py:284
  150.0 1.6 %multiply_bitcast_fusion = f32[1,288,256]{2,1,0:T(8,128)} fusion(bf16[288,256]{1,0:T(8,128)(2,1)} %reduce-scatter.3.cloned.1.call-done), kind=kLoop, calls=%fused_computation | loop fusion | flops 147456 | bytes 442368 | tf_op jit(solution)/shard_map/broadcast_in_dim | solution.py:288
Async XLA Ops:
  7.2 109.6 %reduce-scatter.5.cloned.1.call-start = ((), (), s32[]{:S(2)}) async-start(), calls=%async_computation.3 | async-start | bytes 442368 | tf_op jit(solution)/shard_map/reduce_scatter | solution.py:285
  7.2 1.3 copy-start
  8.5 1.2 copy-start.1
  9.7 1.2 copy-start.2
  10.9 1.0 copy-start.3
  86.6 63.4 %reduce-scatter.3.cloned.1.call-start = ((), (), s32[]{:S(2)}) async-start(), calls=%async_computation.2 | async-start | bytes 1327104 | tf_op jit(solution)/shard_map/reduce_scatter | solution.py:284
Sparse Core Ops, SparseCore 0:
  86.7 29.9 reduce-scatter.4
  119.1 30.8 reduce-scatter.2
where the time goes:
time: 159 us
  Pallas kernels  74.7 us (47%)
  waiting for transfers between devices  61.9 us (39%)
  between operations  14.1 us (9%)
  local copies, waits for them, and re-layouts  4.71 us (3%)
  other arithmetic  3.09 us (2%)
    pallas_call x1, Pallas kernels, local(): pl.pallas_call(functools.partial(kernel, (micros, chunks, height, width,...  74.7 us
    reduce_scatter x1, waiting for transfers between devices, local(): lax.psum_scatter(hold_space, 'dp', scatter_dimension=0, tiled=True)  31.9 us
    reduce_scatter x1, waiting for transfers between devices, local(): lax.psum_scatter(hold_time, 'dp', scatter_dimension=0, tiled=True)  29.4 us
    unnamed x8, local copies, waits for them, and re-layouts  4.71 us
  transfers between devices with their start and end apart: 2, of which 2 were waited for; matrix products, arithmetic and copies ran while one was open for 1% of the time, Pallas kernels for 0%

commit v1 on v0

--- a/solution.py
+++ b/solution.py
@@ -34,14 +34,17 @@
 
 def kernel(
     dims,
+    lat_hbm, cot_hbm, ws_hbm, wt_hbm,
+    ds_ref, dt_ref,
     lat_ref, cot_ref, ws_ref, wt_ref,
-    ds_ref, dt_ref,
     fwd_in, fwd_out, bwd_in, bwd_out,
     slope1, slope2, s1_t, s2_t, ws_t, wt_t,
     cols1, cols2, grads1, grads2, s2_prev, g_next, mixed, acc,
-    f_send, f_recv, b_send, b_recv,
+    pair_out, pair_in, chip_out, chip_in,
+    load_sem, f_send, f_recv, b_send, b_recv,
+    p_send, p_recv, c_send, c_recv,
 ):
-    micros, chunks, height, width, ch, sections = dims
+    micros, chunks, height, width, ch, sections, replicas, grad_scale = dims
     rows = height * PER * width
     line = PER * width
     total = micros * chunks
@@ -49,7 +52,34 @@
     first = sec == 0
     last = sec == sections - 1
 
+    dp = lax.axis_index("dp")
+    core, chip = dp % 2, dp // 2
+    chips = replicas // 2
+    n_space, n_time = 9 * ch // replicas, 3 * ch // replicas
+
+    loads = [
+        pltpu.make_async_copy(source, target, load_sem.at[at])
+        for at, (source, target) in enumerate(
+            ((ws_hbm, ws_ref), (wt_hbm, wt_ref), (lat_hbm, lat_ref), (cot_hbm, cot_ref))
+        )
+    ]
+
+    @pl.when(first)
+    def _():
+        loads[2].start()
+
+    loads[0].start()
+    loads[1].start()
+
+    @pl.when(last)
+    def _():
+        loads[3].start()
+
     barrier = pltpu.get_barrier_semaphore()
+    pl.semaphore_signal(barrier, inc=1, device_id={"dp": dp + 1 - 2 * core}, device_id_type=MESH)
+    for o in range(1, chips):
+        peer = 2 * ((chip + o) % chips) + core
+        pl.semaphore_signal(barrier, inc=1, device_id={"dp": peer}, device_id_type=MESH)
 
     @pl.when(jnp.logical_not(first))
     def _():
@@ -71,11 +101,22 @@
 
     @pl.when(first | last)
     def _():
-        pl.semaphore_wait(barrier, 1)
+        pl.semaphore_wait(barrier, 1 + chips)
 
     @pl.when(jnp.logical_not(first | last))
     def _():
-        pl.semaphore_wait(barrier, 2)
+        pl.semaphore_wait(barrier, 2 + chips)
+
+    @pl.when(first)
+    def _():
+        loads[2].wait()
+
+    loads[0].wait()
+    loads[1].wait()
+
+    @pl.when(last)
+    def _():
+        loads[3].wait()
 
     def f_copy(k):
         return pltpu.make_async_remote_copy(
@@ -186,12 +227,12 @@
                 for other in range(1, chunks):
                     part += dot(s1_t[m * chunks + other], grads1[other, top : top + rows, :])
                 for dc in range(3):
-                    acc[dr * 3 + dc] += part[:, dc * ch : (dc + 1) * ch]
+                    acc[(dr * 3 + dc) * ch : (dr * 3 + dc + 1) * ch, :] += part[:, dc * ch : (dc + 1) * ch]
             part = dot(s2_t[m * chunks], grads2[0])
             for other in range(1, chunks):
                 part += dot(s2_t[m * chunks + other], grads2[other])
             for tap in range(3):
-                acc[9 + tap] += part[:, tap * ch : (tap + 1) * ch]
+                acc[(9 + tap) * ch : (10 + tap) * ch, :] += part[:, tap * ch : (tap + 1) * ch]
 
     lag = chunks - 1 + 2 * (sections - 1)
 
@@ -219,10 +260,44 @@
 
     lax.fori_loop(0, lag + total, tick, 0)
 
-    for tap in range(9):
-        ds_ref[tap * ch : (tap + 1) * ch, :] = acc[tap].astype(jnp.bfloat16)
-    for tap in range(3):
-        dt_ref[tap * ch : (tap + 1) * ch, :] = acc[9 + tap].astype(jnp.bfloat16)
+    def piece(d):
+        space = acc[pl.ds(pl.multiple_of(d * n_space, 8), n_space), :]
+        time = acc[pl.ds(pl.multiple_of(9 * ch + d * n_time, 8), n_time), :]
+        return jnp.concatenate([space, time], axis=0)
+
+    def pair_copy(p):
+        return pltpu.make_async_remote_copy(
+            src_ref=pair_out.at[p], dst_ref=pair_in.at[p],
+            send_sem=p_send.at[p], recv_sem=p_recv.at[p],
+            device_id={"dp": dp + 1 - 2 * core}, device_id_type=MESH,
+        )
+
+    def chip_copy(p, slot):
+        return pltpu.make_async_remote_copy(
+            src_ref=chip_out.at[p], dst_ref=chip_in.at[slot],
+            send_sem=c_send.at[p], recv_sem=c_recv.at[slot],
+            device_id={"dp": 2 * p + core}, device_id_type=MESH,
+        )
+
+    order = [(chip + o) % chips for o in range(1, chips)]
+    for p in order + [chip]:
+        pair_out[p] = piece(2 * p + 1 - core).astype(jnp.bfloat16)
+        pair_copy(p).start()
+    for p in order:
+        pair_copy(p).wait_recv()
+        chip_out[p] = (piece(2 * p + core) + pair_in[p].astype(jnp.float32)).astype(jnp.bfloat16)
+        chip_copy(p, chip).start()
+    pair_copy(chip).wait_recv()
+    share = piece(dp) + pair_in[chip].astype(jnp.float32)
+    for p in order:
+        chip_copy(p, p).wait_recv()
+        share += chip_in[p].astype(jnp.float32)
+    ds_ref[...] = grad_scale * share[:n_space]
+    dt_ref[...] = grad_scale * share[n_space:]
+    for p in order + [chip]:
+        pair_copy(p).wait_send()
+    for p in order:
+        chip_copy(p, chip).wait_send()
 
     @pl.when(jnp.logical_not(last))
     def _():
@@ -245,15 +320,25 @@
     total = micros * chunks
     vmem = pl.BlockSpec(memory_space=pltpu.VMEM)
     bf, f32 = jnp.bfloat16, jnp.float32
-    hold_space, hold_time = pl.pallas_call(
-        functools.partial(kernel, (micros, chunks, height, width, ch, sections)),
+    chips = replicas // 2
+    share = 12 * ch // replicas
+    cells = micros * replicas * crops * frames * height * width
+    grad_scale = 1.0 / math.sqrt(cells)
+    grad_space, grad_time = pl.pallas_call(
+        functools.partial(
+            kernel, (micros, chunks, height, width, ch, sections, replicas, grad_scale)
+        ),
         out_shape=(
-            jax.ShapeDtypeStruct((9 * ch, ch), bf),
-            jax.ShapeDtypeStruct((3 * ch, ch), bf),
+            jax.ShapeDtypeStruct((9 * ch // replicas, ch), f32),
+            jax.ShapeDtypeStruct((3 * ch // replicas, ch), f32),
         ),
-        in_specs=[vmem] * 4,
+        in_specs=[pl.BlockSpec(memory_space=pl.ANY)] * 4,
         out_specs=(vmem, vmem),
         scratch_shapes=[
+            pltpu.VMEM((micros, frames, height, width, ch), bf),
+            pltpu.VMEM((micros, frames, height, width, ch), bf),
+            pltpu.VMEM((9 * ch, ch), bf),
+            pltpu.VMEM((3 * ch, ch), bf),
             pltpu.VMEM((total, rows, ch), bf),
             pltpu.VMEM((total, rows, ch), bf),
             pltpu.VMEM((total, rows, ch), bf),
@@ -271,21 +356,26 @@
             pltpu.VMEM((height, PER, width, ch), f32),
             pltpu.VMEM((height, PER, width, ch), f32),
             pltpu.VMEM((height, PER, width, ch), f32),
-            pltpu.VMEM((12, ch, ch), f32),
+            pltpu.VMEM((12 * ch, ch), f32),
+            pltpu.VMEM((chips, share, ch), bf),
+            pltpu.VMEM((chips, share, ch), bf),
+            pltpu.VMEM((chips, share, ch), bf),
+            pltpu.VMEM((chips, share, ch), bf),
+            pltpu.SemaphoreType.DMA((4,)),
             pltpu.SemaphoreType.DMA((total,)),
             pltpu.SemaphoreType.DMA((total,)),
             pltpu.SemaphoreType.DMA((total,)),
             pltpu.SemaphoreType.DMA((total,)),
+            pltpu.SemaphoreType.DMA((chips,)),
+            pltpu.SemaphoreType.DMA((chips,)),
+            pltpu.SemaphoreType.DMA((chips,)),
+            pltpu.SemaphoreType.DMA((chips,)),
         ],
         compiler_params=pltpu.CompilerParams(
             collective_id=0, has_side_effects=True, vmem_limit_bytes=48 * 1024 * 1024
         ),
     )(latents[:, 0], cotangent[:, 0], spatial_kernels[0], temporal_kernels[0])
-    share_space = lax.psum_scatter(hold_space, "dp", scatter_dimension=0, tiled=True).astype(f32)
-    share_time = lax.psum_scatter(hold_time, "dp", scatter_dimension=0, tiled=True).astype(f32)
-    cells = micros * replicas * crops * frames * height * width
-    grad_scale = 1.0 / math.sqrt(cells)
-    return ((grad_scale * share_space)[None], (grad_scale * share_time)[None])
+    return (grad_space[None], grad_time[None])
 
 
 def solution(mesh):

time: 159 us -> 100 us (0.63)
  the two profiles are of different devices: /device:TPU:0 before, /device:TPU:9 now
where the time goes in v1:
time: 100 us; the launch traced here: 99.7 us
  Pallas kernels  93 us (93%)
  local copies, waits for them, and re-layouts  6.06 us (6%)
    pallas_call x1, Pallas kernels, local(): pl.pallas_call(functools.partial(kernel, (micros, chunks, height, width,...  93 us
    unnamed x10, local copies, waits for them, and re-layouts  6.06 us

profile of v1, /device:TPU:9, one launch (start us, length us, event | category | flops | bytes accessed | tf_op | source)
XLA Modules:
  0.0 99.7 jit_solution(4751016244923320409)
XLA Ops:
  0.6 0.0 copy-start
  0.6 1.3 %copy-done = bf16[1,2304,256]{2,1,0:T(8,128)(2,1)S(1)} copy-done((bf16[1,2304,256]{2,1,0:T(8,128)(2,1)S(1)}, bf16[1,2304,256]{2,1,0:T(8,128)(2,1)}, u32[]{:S(2)}) %copy-start) | copy-done | bytes 1179672
  1.9 0.0 copy-start.1
  1.9 1.2 %copy-done.1 = bf16[4,1,4,16,8,256]{5,4,3,2,1,0:T(8,128)(2,1)S(1)} copy-done((bf16[4,1,4,16,8,256]{5,4,3,2,1,0:T(8,128)(2,1)S(1)}, bf16[4,1,4,16,8,256]{5,4,3,2,1,0:T(8,128)(2,1)}, u32[]{:S(2)}) %copy-start.1) | copy-done | bytes 1048600
  3.1 0.0 copy-start.2
  3.1 1.2 %copy-done.2 = bf16[4,1,4,16,8,256]{5,4,3,2,1,0:T(8,128)(2,1)S(1)} copy-done((bf16[4,1,4,16,8,256]{5,4,3,2,1,0:T(8,128)(2,1)S(1)}, bf16[4,1,4,16,8,256]{5,4,3,2,1,0:T(8,128)(2,1)}, u32[]{:S(2)}) %copy-start.2) | copy-done | bytes 1048600
  4.4 0.0 copy-start.3
  4.4 1.0 copy-done.3
  5.3 93.0 %shard_map.59 = (f32[288,256]{1,0:T(8,128)S(1)}, f32[96,256]{1,0:T(8,128)S(1)}) custom-call(bf16[4,4,16,8,256]{4,3,2,1,0:T(8,128)(2,1)S(1)} %bitcast.7, bf16[4,4,16,8,256]{4,3,2,1,0:T(8,128)(2,1)S(1)} %bitcast.8, bf16[2304,256]{1,0:T(8,128)(2,1)S(1)} %bitcast.6, bf16[768,256]{1,0:T(8,128)(2,1)S(1)} %bitcast.9), custom_call_target="tpu_custom_call" | custom-call | tf_op jit(solution)/shard_map/pallas_call | solution.py:327
  98.3 0.7 copy.8
  99.1 0.6 copy.9
Async XLA Ops:
  0.6 1.3 %copy-start = (bf16[1,2304,256]{2,1,0:T(8,128)(2,1)S(1)}, bf16[1,2304,256]{2,1,0:T(8,128)(2,1)}, u32[]{:S(2)}) copy-start(bf16[1,2304,256]{2,1,0:T(8,128)(2,1)} %param.6) | copy-start | bytes 3538948
  1.9 1.2 %copy-start.1 = (bf16[4,1,4,16,8,256]{5,4,3,2,1,0:T(8,128)(2,1)S(1)}, bf16[4,1,4,16,8,256]{5,4,3,2,1,0:T(8,128)(2,1)}, u32[]{:S(2)}) copy-start(bf16[4,1,4,16,8,256]{5,4,3,2,1,0:T(8,128)(2,1)} %param.4) | copy-start | bytes 3145732
  3.1 1.2 %copy-start.2 = (bf16[4,1,4,16,8,256]{5,4,3,2,1,0:T(8,128)(2,1)S(1)}, bf16[4,1,4,16,8,256]{5,4,3,2,1,0:T(8,128)(2,1)}, u32[]{:S(2)}) copy-start(bf16[4,1,4,16,8,256]{5,4,3,2,1,0:T(8,128)(2,1)} %param.5) | copy-start | bytes 3145732
  4.4 1.0 copy-start.3

commit v2 on v1

--- a/solution.py
+++ b/solution.py
@@ -10,6 +10,7 @@
 
 MESH = pl.DeviceIdType.MESH
 PER = 2
+CUT = 2
 
 
 def slope_of(value, sig):
@@ -48,6 +49,8 @@
     rows = height * PER * width
     line = PER * width
     total = micros * chunks
+    tall = height // CUT
+    part_rows = rows // CUT
     sec = lax.axis_index("section")
     first = sec == 0
     last = sec == sections - 1
@@ -135,7 +138,9 @@
     def arrange(source, m, c, target, k):
         for f in range(PER):
             mixed[:, f] = source[m, c * PER + f].astype(jnp.float32)
-        target[k] = mixed[...].reshape(rows, ch).astype(jnp.bfloat16)
+        for h in range(CUT):
+            piece_in = mixed[h * tall : (h + 1) * tall].reshape(part_rows, ch)
+            target[CUT * k + h] = piece_in.astype(jnp.bfloat16)
 
     def forward(k):
         m, c = k // chunks, k % chunks
@@ -144,42 +149,54 @@
         def _():
             arrange(lat_ref, m, c, fwd_in, k)
 
-        @pl.when(jnp.logical_not(first))
-        def _():
-            f_copy(k).wait_recv()
-
-        x = fwd_in[k].astype(jnp.float32)
-        u = x * inv_rms_of(x)
-        sig = jax.nn.sigmoid(u)
-        s1 = u * sig
-        slope1[k] = slope_of(u, sig)
-        s1b = s1.astype(jnp.bfloat16)
-        cols1[line : line + rows, 0:ch] = column_shift(s1, width, -1).astype(jnp.bfloat16)
-        cols1[line : line + rows, ch : 2 * ch] = s1b
-        cols1[line : line + rows, 2 * ch : 3 * ch] = column_shift(s1, width, 1).astype(jnp.bfloat16)
-        v = dot(cols1[0:rows, :], ws_ref[0 : 3 * ch, :])
-        v += dot(cols1[line : line + rows, :], ws_ref[3 * ch : 6 * ch, :])
-        v += dot(cols1[2 * line : 2 * line + rows, :], ws_ref[6 * ch : 9 * ch, :])
-        sig2 = jax.nn.sigmoid(v)
-        s2 = v * sig2
-        slope2[k] = slope_of(v, sig2)
-        s2b = s2.astype(jnp.bfloat16)
-
-        @pl.when(jnp.logical_not(last))
-        def _():
-            now = s2.reshape(height, PER, width, ch)
-            before = jnp.where(c == 0, 0.0, s2_prev[...])
-            shifted = jnp.concatenate([before[:, 1:], now[:, :1]], axis=1)
-            cols2[:, 0:ch] = before.reshape(rows, ch).astype(jnp.bfloat16)
-            cols2[:, ch : 2 * ch] = shifted.reshape(rows, ch).astype(jnp.bfloat16)
-            cols2[:, 2 * ch : 3 * ch] = s2b
-            s2_prev[...] = now
-            z = dot(cols2[...], wt_ref[...])
-            fwd_out[k] = (x + z).astype(jnp.bfloat16)
-            f_copy(k).start()
-
-        s1_t[k] = s1b.T
-        s2_t[k] = s2b.T
+        s1_parts, s2_parts = [], []
+        for h in range(CUT):
+            q = CUT * k + h
+            top = line + h * part_rows
+
+            @pl.when(jnp.logical_not(first))
+            def _():
+                f_copy(q).wait_recv()
+
+            x = fwd_in[q].astype(jnp.float32)
+            u = x * inv_rms_of(x)
+            sig = jax.nn.sigmoid(u)
+            s1 = u * sig
+            slope1[q] = slope_of(u, sig)
+            s1b = s1.astype(jnp.bfloat16)
+            s1_parts.append(s1b)
+            left, right = column_shift(s1, width, -1), column_shift(s1, width, 1)
+            cols1[top : top + part_rows, 0:ch] = left.astype(jnp.bfloat16)
+            cols1[top : top + part_rows, ch : 2 * ch] = s1b
+            cols1[top : top + part_rows, 2 * ch : 3 * ch] = right.astype(jnp.bfloat16)
+        for h in range(CUT):
+            q = CUT * k + h
+            top = h * part_rows
+            v = dot(cols1[top : top + part_rows, :], ws_ref[0 : 3 * ch, :])
+            v += dot(cols1[top + line : top + line + part_rows, :], ws_ref[3 * ch : 6 * ch, :])
+            v += dot(cols1[top + 2 * line : top + 2 * line + part_rows, :], ws_ref[6 * ch : 9 * ch, :])
+            sig2 = jax.nn.sigmoid(v)
+            s2 = v * sig2
+            slope2[q] = slope_of(v, sig2)
+            s2b = s2.astype(jnp.bfloat16)
+            s2_parts.append(s2b)
+
+            @pl.when(jnp.logical_not(last))
+            def _():
+                now = s2.reshape(tall, PER, width, ch)
+                before = jnp.where(c == 0, 0.0, s2_prev[h * tall : (h + 1) * tall])
+                shifted = jnp.concatenate([before[:, 1:], now[:, :1]], axis=1)
+                cols2[top : top + part_rows, 0:ch] = before.reshape(part_rows, ch).astype(jnp.bfloat16)
+                cols2[top : top + part_rows, ch : 2 * ch] = shifted.reshape(part_rows, ch).astype(jnp.bfloat16)
+                cols2[top : top + part_rows, 2 * ch : 3 * ch] = s2b
+                s2_prev[h * tall : (h + 1) * tall] = now
+                z = dot(cols2[top : top + part_rows, :], wt_ref[...])
+                fwd_out[q] = (fwd_in[q].astype(jnp.float32) + z).astype(jnp.bfloat16)
+                f_copy(q).start()
+
+        for h in range(CUT):
+            s1_t[k, :, h * part_rows : (h + 1) * part_rows] = s1_parts[h].T
+            s2_t[k, :, h * part_rows : (h + 1) * part_rows] = s2_parts[h].T
 
     def backward(j):
         m, c = j // chunks, chunks - 1 - j % chunks
@@ -189,35 +206,43 @@
         def _():
             arrange(cot_ref, m, c, bwd_in, k)
 
-        @pl.when(jnp.logical_not(last))
-        def _():
-            b_copy(k).wait_recv()
-
-        gb = bwd_in[k]
-        g = gb.astype(jnp.float32)
-        now = g.reshape(height, PER, width, ch)
-        after = jnp.where(c == chunks - 1, 0.0, g_next[...])
-        shifted = jnp.concatenate([now[:, 1:], after[:, :1]], axis=1)
-        grads2[c, :, 0:ch] = after.reshape(rows, ch).astype(jnp.bfloat16)
-        grads2[c, :, ch : 2 * ch] = shifted.reshape(rows, ch).astype(jnp.bfloat16)
-        grads2[c, :, 2 * ch : 3 * ch] = gb
-        g_next[...] = now
-        gmid = dot(grads2[c], wt_t[...]) * slope2[k]
-        grads1[c, line : line + rows, 0:ch] = column_shift(gmid, width, 1).astype(jnp.bfloat16)
-        grads1[c, line : line + rows, ch : 2 * ch] = gmid.astype(jnp.bfloat16)
-        grads1[c, line : line + rows, 2 * ch : 3 * ch] = column_shift(gmid, width, -1).astype(jnp.bfloat16)
+        for h in range(CUT):
+            q = CUT * k + h
+            top = h * part_rows
+
+            @pl.when(jnp.logical_not(last))
+            def _():
+                b_copy(q).wait_recv()
+
+            gb = bwd_in[q]
+            now = gb.astype(jnp.float32).reshape(tall, PER, width, ch)
+            after = jnp.where(c == chunks - 1, 0.0, g_next[h * tall : (h + 1) * tall])
+            shifted = jnp.concatenate([now[:, 1:], after[:, :1]], axis=1)
+            grads2[c, top : top + part_rows, 0:ch] = after.reshape(part_rows, ch).astype(jnp.bfloat16)
+            grads2[c, top : top + part_rows, ch : 2 * ch] = shifted.reshape(part_rows, ch).astype(jnp.bfloat16)
+            grads2[c, top : top + part_rows, 2 * ch : 3 * ch] = gb
+            g_next[h * tall : (h + 1) * tall] = now
+            gmid = dot(grads2[c, top : top + part_rows, :], wt_t[...]) * slope2[q]
+            top += line
+            left, right = column_shift(gmid, width, 1), column_shift(gmid, width, -1)
+            grads1[c, top : top + part_rows, 0:ch] = left.astype(jnp.bfloat16)
+            grads1[c, top : top + part_rows, ch : 2 * ch] = gmid.astype(jnp.bfloat16)
+            grads1[c, top : top + part_rows, 2 * ch : 3 * ch] = right.astype(jnp.bfloat16)
 
         @pl.when(jnp.logical_not(first))
         def _():
-            back = dot(grads1[c, 2 * line : 2 * line + rows, :], ws_t[0 : 3 * ch, :])
-            back += dot(grads1[c, line : line + rows, :], ws_t[3 * ch : 6 * ch, :])
-            back += dot(grads1[c, 0:rows, :], ws_t[6 * ch : 9 * ch, :])
-            gu = back * slope1[k]
-            x = fwd_in[k].astype(jnp.float32)
-            inv = inv_rms_of(x)
-            gx = inv * gu - x * (inv * inv * inv) * jnp.mean(gu * x, axis=-1, keepdims=True)
-            bwd_out[k] = (g + gx).astype(jnp.bfloat16)
-            b_copy(k).start()
+            for h in range(CUT):
+                q = CUT * k + h
+                top = h * part_rows
+                back = dot(grads1[c, top + 2 * line : top + 2 * line + part_rows, :], ws_t[0 : 3 * ch, :])
+                back += dot(grads1[c, top + line : top + line + part_rows, :], ws_t[3 * ch : 6 * ch, :])
+                back += dot(grads1[c, top : top + part_rows, :], ws_t[6 * ch : 9 * ch, :])
+                gu = back * slope1[q]
+                x = fwd_in[q].astype(jnp.float32)
+                inv = inv_rms_of(x)
+                gx = inv * gu - x * (inv * inv * inv) * jnp.mean(gu * x, axis=-1, keepdims=True)
+                bwd_out[q] = (bwd_in[q].astype(jnp.float32) + gx).astype(jnp.bfloat16)
+                b_copy(q).start()
 
         @pl.when(c == 0)
         def _():
@@ -301,12 +326,12 @@
 
     @pl.when(jnp.logical_not(last))
     def _():
-        for k in range(total):
+        for k in range(CUT * total):
             f_copy(k).wait_send()
 
     @pl.when(jnp.logical_not(first))
     def _():
-        for k in range(total):
+        for k in range(CUT * total):
             b_copy(k).wait_send()
 
 
@@ -332,19 +357,19 @@
             jax.ShapeDtypeStruct((9 * ch // replicas, ch), f32),
             jax.ShapeDtypeStruct((3 * ch // replicas, ch), f32),
         ),
-        in_specs=[pl.BlockSpec(memory_space=pl.ANY)] * 4,
+        in_specs=[pl.BlockSpec(memory_space=pltpu.HBM)] * 4,
         out_specs=(vmem, vmem),
         scratch_shapes=[
             pltpu.VMEM((micros, frames, height, width, ch), bf),
             pltpu.VMEM((micros, frames, height, width, ch), bf),
             pltpu.VMEM((9 * ch, ch), bf),
             pltpu.VMEM((3 * ch, ch), bf),
-            pltpu.VMEM((total, rows, ch), bf),
-            pltpu.VMEM((total, rows, ch), bf),
-            pltpu.VMEM((total, rows, ch), bf),
-            pltpu.VMEM((total, rows, ch), bf),
-            pltpu.VMEM((total, rows, ch), f32),
-            pltpu.VMEM((total, rows, ch), f32),
+            pltpu.VMEM((CUT * total, rows // CUT, ch), bf),
+            pltpu.VMEM((CUT * total, rows // CUT, ch), bf),
+            pltpu.VMEM((CUT * total, rows // CUT, ch), bf),
+            pltpu.VMEM((CUT * total, rows // CUT, ch), bf),
+            pltpu.VMEM((CUT * total, rows // CUT, ch), f32),
+            pltpu.VMEM((CUT * total, rows // CUT, ch), f32),
             pltpu.VMEM((total, ch, rows), bf),
             pltpu.VMEM((total, ch, rows), bf),
             pltpu.VMEM((9 * ch, ch), bf),
@@ -362,10 +387,10 @@
             pltpu.VMEM((chips, share, ch), bf),
             pltpu.VMEM((chips, share, ch), bf),
             pltpu.SemaphoreType.DMA((4,)),
-            pltpu.SemaphoreType.DMA((total,)),
-            pltpu.SemaphoreType.DMA((total,)),
-            pltpu.SemaphoreType.DMA((total,)),
-            pltpu.SemaphoreType.DMA((total,)),
+            pltpu.SemaphoreType.DMA((CUT * total,)),
+            pltpu.SemaphoreType.DMA((CUT * total,)),
+            pltpu.SemaphoreType.DMA((CUT * total,)),
+            pltpu.SemaphoreType.DMA((CUT * total,)),
             pltpu.SemaphoreType.DMA((chips,)),
             pltpu.SemaphoreType.DMA((chips,)),
             pltpu.SemaphoreType.DMA((chips,)),

time: 100 us -> 99.9 us (level)
  no operation moved by 1% of the time
where the time goes in v2:
time: 99.9 us; the launch traced here: 99.6 us
  Pallas kernels  92.9 us (93%)
  local copies, waits for them, and re-layouts  6.06 us (6%)
    pallas_call x1, Pallas kernels, local(): pl.pallas_call(functools.partial(kernel, (micros, chunks, height, width,...  92.9 us
    unnamed x10, local copies, waits for them, and re-layouts  6.06 us

profile of v2, /device:TPU:9, one launch (start us, length us, event | category | flops | bytes accessed | tf_op | source)
XLA Modules:
  0.0 99.6 jit_solution(7115926852390087723)
XLA Ops:
  0.6 0.0 copy-start
  0.6 1.3 %copy-done = bf16[1,2304,256]{2,1,0:T(8,128)(2,1)S(1)} copy-done((bf16[1,2304,256]{2,1,0:T(8,128)(2,1)S(1)}, bf16[1,2304,256]{2,1,0:T(8,128)(2,1)}, u32[]{:S(2)}) %copy-start) | copy-done | bytes 1179672
  1.9 0.0 copy-start.1
  1.9 1.2 %copy-done.1 = bf16[4,1,4,16,8,256]{5,4,3,2,1,0:T(8,128)(2,1)S(1)} copy-done((bf16[4,1,4,16,8,256]{5,4,3,2,1,0:T(8,128)(2,1)S(1)}, bf16[4,1,4,16,8,256]{5,4,3,2,1,0:T(8,128)(2,1)}, u32[]{:S(2)}) %copy-start.1) | copy-done | bytes 1048600
  3.1 0.0 copy-start.2
  3.1 1.2 %copy-done.2 = bf16[4,1,4,16,8,256]{5,4,3,2,1,0:T(8,128)(2,1)S(1)} copy-done((bf16[4,1,4,16,8,256]{5,4,3,2,1,0:T(8,128)(2,1)S(1)}, bf16[4,1,4,16,8,256]{5,4,3,2,1,0:T(8,128)(2,1)}, u32[]{:S(2)}) %copy-start.2) | copy-done | bytes 1048600
  4.4 0.0 copy-start.3
  4.4 1.0 copy-done.3
  5.3 92.9 %shard_map.59 = (f32[288,256]{1,0:T(8,128)S(1)}, f32[96,256]{1,0:T(8,128)S(1)}) custom-call(bf16[4,4,16,8,256]{4,3,2,1,0:T(8,128)(2,1)S(1)} %bitcast.7, bf16[4,4,16,8,256]{4,3,2,1,0:T(8,128)(2,1)S(1)} %bitcast.8, bf16[2304,256]{1,0:T(8,128)(2,1)S(1)} %bitcast.6, bf16[768,256]{1,0:T(8,128)(2,1)S(1)} %bitcast.9), custom_call_target="tpu_custom_call" | custom-call | tf_op jit(solution)/shard_map/pallas_call | solution.py:352
  98.3 0.7 copy.8
  99.0 0.6 copy.9
Async XLA Ops:
  0.6 1.3 %copy-start = (bf16[1,2304,256]{2,1,0:T(8,128)(2,1)S(1)}, bf16[1,2304,256]{2,1,0:T(8,128)(2,1)}, u32[]{:S(2)}) copy-start(bf16[1,2304,256]{2,1,0:T(8,128)(2,1)} %param.6) | copy-start | bytes 3538948
  1.9 1.2 %copy-start.1 = (bf16[4,1,4,16,8,256]{5,4,3,2,1,0:T(8,128)(2,1)S(1)}, bf16[4,1,4,16,8,256]{5,4,3,2,1,0:T(8,128)(2,1)}, u32[]{:S(2)}) copy-start(bf16[4,1,4,16,8,256]{5,4,3,2,1,0:T(8,128)(2,1)} %param.4) | copy-start | bytes 3145732
  3.1 1.2 %copy-start.2 = (bf16[4,1,4,16,8,256]{5,4,3,2,1,0:T(8,128)(2,1)S(1)}, bf16[4,1,4,16,8,256]{5,4,3,2,1,0:T(8,128)(2,1)}, u32[]{:S(2)}) copy-start(bf16[4,1,4,16,8,256]{5,4,3,2,1,0:T(8,128)(2,1)} %param.5) | copy-start | bytes 3145732
  4.4 1.0 copy-start.3

commit v3 on v2

--- a/solution.py
+++ b/solution.py
@@ -96,7 +96,7 @@
     edge_rows = jnp.zeros((line, 3 * ch), jnp.bfloat16)
     cols1[0:line, :] = edge_rows
     cols1[line + rows : 2 * line + rows, :] = edge_rows
-    for slot in range(chunks):
+    for slot in range(total):
         grads1[slot, 0:line, :] = edge_rows
         grads1[slot, line + rows : 2 * line + rows, :] = edge_rows
     s2_prev[...] = jnp.zeros_like(s2_prev)
@@ -198,6 +198,18 @@
             s1_t[k, :, h * part_rows : (h + 1) * part_rows] = s1_parts[h].T
             s2_t[k, :, h * part_rows : (h + 1) * part_rows] = s2_parts[h].T
 
+    def kernel_terms(m):
+        spans = [m * chunks + c for c in range(chunks)]
+        for dr in range(3):
+            top = (2 - dr) * line
+            part = sum(dot(s1_t[k], grads1[k, top : top + rows, :]) for k in spans)
+            for dc in range(3):
+                tap = dr * 3 + dc
+                acc[tap * ch : (tap + 1) * ch, :] += part[:, dc * ch : (dc + 1) * ch]
+        part = sum(dot(s2_t[k], grads2[k]) for k in spans)
+        for tap in range(3):
+            acc[(9 + tap) * ch : (10 + tap) * ch, :] += part[:, tap * ch : (tap + 1) * ch]
+
     def backward(j):
         m, c = j // chunks, chunks - 1 - j % chunks
         k = m * chunks + c
@@ -218,25 +230,25 @@
             now = gb.astype(jnp.float32).reshape(tall, PER, width, ch)
             after = jnp.where(c == chunks - 1, 0.0, g_next[h * tall : (h + 1) * tall])
             shifted = jnp.concatenate([now[:, 1:], after[:, :1]], axis=1)
-            grads2[c, top : top + part_rows, 0:ch] = after.reshape(part_rows, ch).astype(jnp.bfloat16)
-            grads2[c, top : top + part_rows, ch : 2 * ch] = shifted.reshape(part_rows, ch).astype(jnp.bfloat16)
-            grads2[c, top : top + part_rows, 2 * ch : 3 * ch] = gb
+            grads2[k, top : top + part_rows, 0:ch] = after.reshape(part_rows, ch).astype(jnp.bfloat16)
+            grads2[k, top : top + part_rows, ch : 2 * ch] = shifted.reshape(part_rows, ch).astype(jnp.bfloat16)
+            grads2[k, top : top + part_rows, 2 * ch : 3 * ch] = gb
             g_next[h * tall : (h + 1) * tall] = now
-            gmid = dot(grads2[c, top : top + part_rows, :], wt_t[...]) * slope2[q]
+            gmid = dot(grads2[k, top : top + part_rows, :], wt_t[...]) * slope2[q]
             top += line
             left, right = column_shift(gmid, width, 1), column_shift(gmid, width, -1)
-            grads1[c, top : top + part_rows, 0:ch] = left.astype(jnp.bfloat16)
-            grads1[c, top : top + part_rows, ch : 2 * ch] = gmid.astype(jnp.bfloat16)
-            grads1[c, top : top + part_rows, 2 * ch : 3 * ch] = right.astype(jnp.bfloat16)
+            grads1[k, top : top + part_rows, 0:ch] = left.astype(jnp.bfloat16)
+            grads1[k, top : top + part_rows, ch : 2 * ch] = gmid.astype(jnp.bfloat16)
+            grads1[k, top : top + part_rows, 2 * ch : 3 * ch] = right.astype(jnp.bfloat16)
 
         @pl.when(jnp.logical_not(first))
         def _():
             for h in range(CUT):
                 q = CUT * k + h
                 top = h * part_rows
-                back = dot(grads1[c, top + 2 * line : top + 2 * line + part_rows, :], ws_t[0 : 3 * ch, :])
-                back += dot(grads1[c, top + line : top + line + part_rows, :], ws_t[3 * ch : 6 * ch, :])
-                back += dot(grads1[c, top : top + part_rows, :], ws_t[6 * ch : 9 * ch, :])
+                back = dot(grads1[k, top + 2 * line : top + 2 * line + part_rows, :], ws_t[0 : 3 * ch, :])
+                back += dot(grads1[k, top + line : top + line + part_rows, :], ws_t[3 * ch : 6 * ch, :])
+                back += dot(grads1[k, top : top + part_rows, :], ws_t[6 * ch : 9 * ch, :])
                 gu = back * slope1[q]
                 x = fwd_in[q].astype(jnp.float32)
                 inv = inv_rms_of(x)
@@ -244,20 +256,9 @@
                 bwd_out[q] = (bwd_in[q].astype(jnp.float32) + gx).astype(jnp.bfloat16)
                 b_copy(q).start()
 
-        @pl.when(c == 0)
-        def _():
-            for dr in range(3):
-                top = (2 - dr) * line
-                part = dot(s1_t[m * chunks], grads1[0, top : top + rows, :])
-                for other in range(1, chunks):
-                    part += dot(s1_t[m * chunks + other], grads1[other, top : top + rows, :])
-                for dc in range(3):
-                    acc[(dr * 3 + dc) * ch : (dr * 3 + dc + 1) * ch, :] += part[:, dc * ch : (dc + 1) * ch]
-            part = dot(s2_t[m * chunks], grads2[0])
-            for other in range(1, chunks):
-                part += dot(s2_t[m * chunks + other], grads2[other])
-            for tap in range(3):
-                acc[(9 + tap) * ch : (10 + tap) * ch, :] += part[:, tap * ch : (tap + 1) * ch]
+        @pl.when(first & (c == 0))
+        def _():
+            kernel_terms(m)
 
     lag = chunks - 1 + 2 * (sections - 1)
 
@@ -284,6 +285,14 @@
         return carry
 
     lax.fori_loop(0, lag + total, tick, 0)
+
+    @pl.when(jnp.logical_not(first))
+    def _():
+        def late(m, carry):
+            kernel_terms(m)
+            return carry
+
+        lax.fori_loop(0, micros, late, 0)
 
     def piece(d):
         space = acc[pl.ds(pl.multiple_of(d * n_space, 8), n_space), :]
@@ -376,8 +385,8 @@
             pltpu.VMEM((3 * ch, ch), bf),
             pltpu.VMEM((rows + 2 * line, 3 * ch), bf),
             pltpu.VMEM((rows, 3 * ch), bf),
-            pltpu.VMEM((chunks, rows + 2 * line, 3 * ch), bf),
-            pltpu.VMEM((chunks, rows, 3 * ch), bf),
+            pltpu.VMEM((total, rows + 2 * line, 3 * ch), bf),
+            pltpu.VMEM((total, rows, 3 * ch), bf),
             pltpu.VMEM((height, PER, width, ch), f32),
             pltpu.VMEM((height, PER, width, ch), f32),
             pltpu.VMEM((height, PER, width, ch), f32),
@@ -397,7 +406,7 @@
             pltpu.SemaphoreType.DMA((chips,)),
         ],
         compiler_params=pltpu.CompilerParams(
-            collective_id=0, has_side_effects=True, vmem_limit_bytes=48 * 1024 * 1024
+            collective_id=0, has_side_effects=True, vmem_limit_bytes=62 * 1024 * 1024
         ),
     )(latents[:, 0], cotangent[:, 0], spatial_kernels[0], temporal_kernels[0])
     return (grad_space[None], grad_time[None])

time: 99.9 us -> 97.4 us (0.975)
  local copies, waits for them, and re-layouts: 6.06 us -> 3.23 us
    unnamed x10 -> x2, local copies, waits for them, and re-layouts: 6.06 us -> 3.23 us
where the time goes in v3:
time: 97.4 us; the launch traced here: 97.3 us
  Pallas kernels  93.4 us (96%)
  local copies, waits for them, and re-layouts  3.23 us (3%)
    pallas_call x1, Pallas kernels, local(): pl.pallas_call(functools.partial(kernel, (micros, chunks, height, width,...  93.4 us
    unnamed x2, local copies, waits for them, and re-layouts  3.23 us

profile of v3, /device:TPU:9, one launch (start us, length us, event | category | flops | bytes accessed | tf_op | source)
XLA Modules:
  0.0 97.3 jit_solution(3358926706484184450)
XLA Ops:
  0.6 93.4 %shard_map.59 = (f32[288,256]{1,0:T(8,128)}, f32[96,256]{1,0:T(8,128)}) custom-call(bf16[4,4,16,8,256]{4,3,2,1,0:T(8,128)(2,1)} %bitcast.7, bf16[4,4,16,8,256]{4,3,2,1,0:T(8,128)(2,1)} %bitcast.8, bf16[2304,256]{1,0:T(8,128)(2,1)} %bitcast.6, bf16[768,256]{1,0:T(8,128)(2,1)} %bitcast.9), custom_call_target="tpu_custom_call" | custom-call | tf_op jit(solution)/shard_map/pallas_call | solution.py:361
  94.0 1.7 %copy.8 = f32[1,288,256]{2,1,0:T(8,128)} copy(f32[1,288,256]{2,1,0:T(8,128)} %bitcast.10) | data formatting | bytes 589824
  95.7 1.5 %copy.9 = f32[1,96,256]{2,1,0:T(8,128)} copy(f32[1,96,256]{2,1,0:T(8,128)} %bitcast.11) | data formatting | bytes 196608

commit v4 on v3

--- a/solution.py
+++ b/solution.py
@@ -10,7 +10,7 @@
 
 MESH = pl.DeviceIdType.MESH
 PER = 2
-CUT = 2
+CUT = 1
 
 
 def slope_of(value, sig):

time: 97.4 us -> 97.9 us (level)
  no operation moved by 1% of the time
where the time goes in v4:
time: 97.9 us; the launch traced here: 97.7 us
  Pallas kernels  93.8 us (96%)
  local copies, waits for them, and re-layouts  3.23 us (3%)
    pallas_call x1, Pallas kernels, local(): pl.pallas_call(functools.partial(kernel, (micros, chunks, height, width,...  93.8 us
    unnamed x2, local copies, waits for them, and re-layouts  3.23 us

profile of v4, /device:TPU:9, one launch (start us, length us, event | category | flops | bytes accessed | tf_op | source)
XLA Modules:
  0.0 97.7 jit_solution(5045211446991313694)
XLA Ops:
  0.6 93.8 %shard_map.59 = (f32[288,256]{1,0:T(8,128)}, f32[96,256]{1,0:T(8,128)}) custom-call(bf16[4,4,16,8,256]{4,3,2,1,0:T(8,128)(2,1)} %bitcast.7, bf16[4,4,16,8,256]{4,3,2,1,0:T(8,128)(2,1)} %bitcast.8, bf16[2304,256]{1,0:T(8,128)(2,1)} %bitcast.6, bf16[768,256]{1,0:T(8,128)(2,1)} %bitcast.9), custom_call_target="tpu_custom_call" | custom-call | tf_op jit(solution)/shard_map/pallas_call | solution.py:361
  94.5 1.7 %copy.8 = f32[1,288,256]{2,1,0:T(8,128)} copy(f32[1,288,256]{2,1,0:T(8,128)} %bitcast.10) | data formatting | bytes 589824
  96.2 1.5 %copy.9 = f32[1,96,256]{2,1,0:T(8,128)} copy(f32[1,96,256]{2,1,0:T(8,128)} %bitcast.11) | data formatting | bytes 196608
